TPU v7x, 32 devices: a whole 2x2x4 slice. The times are simulated.
32 devices in a mesh: groups: 2 (over y), tensor: 4 (over z), dp: 2 (over x), pipe: 2 (over core).
Axes of the slice: x: 2, y: 2, z: 4, core: 2. Of those that a mesh axis runs over, the one named last changes fastest.
Arguments:
- tokens: bfloat16 [4, 256, 4096], P(('groups', 'dp'), 'tensor'), parts along dimension 0, may hold values from -6 to 6
- gate_preactivation: bfloat16 [4, 14336, 256], P(('groups', 'dp'), ('tensor', 'pipe')), parts along dimension 0, may hold values from -6 to 6
- up_preactivation: bfloat16 [4, 14336, 256], P(('groups', 'dp'), ('tensor', 'pipe')), parts along dimension 0, may hold values from -6 to 6
- hidden_gradient: bfloat16 [4, 14336, 256], P(('groups', 'dp'), ('tensor', 'pipe')), parts along dimension 0, may hold values from -1 to 1
- gate_merged_weight: bfloat16 [14336, 4096], P(('tensor', 'pipe')), may hold values from -0.375 to 0.375
- up_merged_weight: bfloat16 [14336, 4096], P(('tensor', 'pipe')), may hold values from -0.375 to 0.375
- gate_down_factor: bfloat16 [64, 4096], P(None, 'pipe'), may hold values from -0.01171875 to 0.01171875
- up_down_factor: bfloat16 [64, 4096], P(None, 'pipe'), may hold values from -0.01171875 to 0.01171875
- gate_up_factor: bfloat16 [14336, 64], P(('tensor', 'pipe')), may hold values from -0.005859375 to 0.005859375
- up_up_factor: bfloat16 [14336, 64], P(('tensor', 'pipe')), may hold values from -0.005859375 to 0.005859375
Outputs:
- input_grad: bfloat16 [4, 256, 4096], P(('groups', 'dp'), ('tensor', 'pipe')), parts along dimension 0
- gate_a_grad: float32 [128, 4096], P('groups', 'pipe'), parts along dimension 0
- up_a_grad: float32 [128, 4096], P('groups', 'pipe'), parts along dimension 0
- gate_b_grad: float32 [28672, 64], P(('groups', 'tensor', 'pipe')), parts along dimension 0
- up_b_grad: float32 [28672, 64], P(('groups', 'tensor', 'pipe')), parts along dimension 0
There are 2 independent parts, one for each index of `groups`. A program takes and returns all parts, laid end to end along the dimension named above; an argument that names none is the same for every part. Nothing has to cross between parts.
All inputs are finite; a program needn't handle non-finite values.
Results may differ from a plain program's by a relative error of at most 0.005.
Values may be sent and summed in bfloat16 or wider, within the bound.
A program may use at most 128 MiB of HBM per device.

v0:
```python
import jax
import jax.numpy as jnp
from jax import lax
from jax.sharding import PartitionSpec as P


def body(
    tokens,
    gate_preactivation,
    up_preactivation,
    hidden_gradient,
    gate_merged_weight,
    up_merged_weight,
    gate_down_factor,
    up_down_factor,
    gate_up_factor,
    up_up_factor,
):
    highest_precision = lax.Precision.HIGHEST
    contract_leading = (((0,), (0,)), ((), ()))
    contract_last = (((1,), (1,)), ((), ()))
    gate_vals = gate_preactivation[0].astype(jnp.float32)
    up_vals = up_preactivation[0].astype(jnp.float32)
    grad_vals = hidden_gradient[0].astype(jnp.float32)
    sigmoid = jax.nn.sigmoid(gate_vals)
    gate_gradient = (grad_vals * up_vals * sigmoid * (1.0 + gate_vals * (1.0 - sigmoid))).astype(
        jnp.bfloat16
    )
    up_gradient = (grad_vals * gate_vals * sigmoid).astype(jnp.bfloat16)
    own_rows = tokens[0]
    gate_backward = lax.dot_general(
        gate_gradient, gate_up_factor, contract_leading, preferred_element_type=jnp.float32
    )
    up_backward = lax.dot_general(
        up_gradient, up_up_factor, contract_leading, preferred_element_type=jnp.float32
    )
    gate_adapter, up_adapter = (
        lax.all_gather(gate_down_factor, "pipe", axis=1, tiled=True),
        lax.all_gather(up_down_factor, "pipe", axis=1, tiled=True),
    )
    gate_projected = lax.dot_general(
        own_rows, gate_adapter, contract_last, preferred_element_type=jnp.float32
    ).astype(jnp.bfloat16)
    up_projected = lax.dot_general(
        own_rows, up_adapter, contract_last, preferred_element_type=jnp.float32
    ).astype(jnp.bfloat16)
    own_gate = gate_projected
    own_up = up_projected
    gate_projected, up_projected = (
        lax.all_gather(own_gate, "tensor", axis=0, tiled=True),
        lax.all_gather(own_up, "tensor", axis=0, tiled=True),
    )
    gate_b_part = jnp.dot(gate_gradient, gate_projected, preferred_element_type=jnp.float32)
    up_b_part = jnp.dot(up_gradient, up_projected, preferred_element_type=jnp.float32)
    gate_owned, up_owned = (
        lax.psum_scatter(gate_backward, "tensor", scatter_dimension=0, tiled=True),
        lax.psum_scatter(up_backward, "tensor", scatter_dimension=0, tiled=True),
    )
    row_vals = own_rows.astype(jnp.float32)
    gate_a_part = lax.dot_general(
        gate_owned,
        row_vals,
        contract_leading,
        precision=highest_precision,
        preferred_element_type=jnp.float32,
    )
    up_a_part = lax.dot_general(
        up_owned,
        row_vals,
        contract_leading,
        precision=highest_precision,
        preferred_element_type=jnp.float32,
    )
    gate_a_full, up_a_full = lax.psum((gate_a_part, up_a_part), ("tensor", "dp", "pipe"))
    half_hidden_width = gate_down_factor.shape[1]
    offset = lax.axis_index("pipe") * half_hidden_width
    gate_a_grad = lax.dynamic_slice_in_dim(gate_a_full, offset, half_hidden_width, 1)
    up_a_grad = lax.dynamic_slice_in_dim(up_a_full, offset, half_hidden_width, 1)
    gate_b_grad, up_b_grad = lax.psum((gate_b_part, up_b_part), "dp")
    first = lax.dot_general(
        gate_gradient, gate_merged_weight, contract_leading, preferred_element_type=jnp.float32
    )
    second = lax.dot_general(
        up_gradient, up_merged_weight, contract_leading, preferred_element_type=jnp.float32
    )
    input_share = lax.psum_scatter(
        first + second, ("tensor", "pipe"), scatter_dimension=0, tiled=True
    )
    input_grad = input_share.astype(jnp.bfloat16)[None]
    return (input_grad, gate_a_grad, up_a_grad, gate_b_grad, up_b_grad)


def solution(mesh):
    placed = (
        P(("groups", "dp"), "tensor", None),
        P(("groups", "dp"), ("tensor", "pipe"), None),
        P(("groups", "dp"), ("tensor", "pipe"), None),
        P(("groups", "dp"), ("tensor", "pipe"), None),
        P(("tensor", "pipe"), None),
        P(("tensor", "pipe"), None),
        P(None, "pipe"),
        P(None, "pipe"),
        P(("tensor", "pipe"), None),
        P(("tensor", "pipe"), None),
    )
    return jax.shard_map(
        body,
        mesh=mesh,
        in_specs=placed,
        out_specs=(
            P(("groups", "dp"), ("tensor", "pipe"), None),
            P("groups", "pipe"),
            P("groups", "pipe"),
            P(("groups", "tensor", "pipe"), None),
            P(("groups", "tensor", "pipe"), None),
        ),
        check_vma=False,
    )
```

profile of v0, /device:TPU:28, one launch (start us, length us, event | category | flops | bytes accessed | tf_op | source)
XLA Modules:
  0.0 229.2 jit_solution(2608423189240714783)
XLA Ops:
  8.0 0.0 copy-start
  8.0 0.0 copy-start.3
  8.0 0.0 copy-start.4
  8.0 0.0 reduce-scatter.6.cloned.1.call-start
  8.1 2.8 %fusion.8 = (bf16[1792,256]{1,0:T(8,128)(2,1)S(1)}, bf16[1792,256]{1,0:T(8,128)(2,1)S(1)}) fusion(bf16[1,1792,256]{2,1,0:T(8,128)(2,1)} %param.13, bf16[1,1792,256]{2,1,0:T(8,128)(2,1)} %param.11, bf16[1,1792,256]{2,1,0:T(8,128)(2,1)} %param.12), kind=kLoop, calls=%fused_computation.13 | loop fusion | flops 7340032 | bytes 4587520 | tf_op jit(solution)/shard_map/convert_element_type | solution.py:29
  10.8 0.0 copy-done.3
  10.8 1.1 fusion.16
  11.9 0.0 reduce-scatter.6.cloned.1.call-update
  12.0 0.0 reduce-scatter.8.cloned.1.call-start
  12.0 0.0 copy-done.4
  12.0 1.1 fusion.17
  13.1 0.0 reduce-scatter.8.cloned.1.call-update
  13.2 0.0 all-reduce.5.cloned.1.call-start
  13.2 10.7 %fusion.15 = f32[256,4096]{1,0:T(8,128)} fusion(bf16[1792,256]{1,0:T(8,128)(2,1)S(1)} %get-tuple-element.10, bf16[1792,4096]{1,0:T(8,128)(2,1)} %param.14), kind=kOutput, calls=%fused_computation.25 | convolution fusion | flops 3758096384 | bytes 19791872 | tf_op jit(solution)/shard_map/dot_general | solution.py:80
  23.9 5.5 %reduce-scatter.6.cloned.1.call-done = f32[64,64]{1,0:T(8,128)} async-done(((f32[256,64]{1,0:T(8,128)}), f32[64,64]{1,0:T(8,128)}) %reduce-scatter.6.cloned.1.call-update) | async-done | bytes 16400 | tf_op jit(solution)/shard_map/reduce_scatter | solution.py:56
  29.4 0.0 copy-done
  29.4 2.3 %fusion.13 = f32[64,4096]{1,0:T(8,128)} fusion(f32[64,64]{1,0:T(8,128)} %reduce-scatter.6.cloned.1.call-done, bf16[1,64,4096]{2,1,0:T(8,128)(2,1)S(1)} %copy-done), kind=kOutput, calls=%fused_computation.20 | convolution fusion | flops 201326592 | bytes 1589248 | tf_op jit(solution)/shard_map/dot_general | solution.py:60
  31.8 17.9 %reduce-scatter.8.cloned.1.call-done = f32[64,64]{1,0:T(8,128)} async-done(((f32[256,64]{1,0:T(8,128)}), f32[64,64]{1,0:T(8,128)}) %reduce-scatter.8.cloned.1.call-update) | async-done | bytes 16400 | tf_op jit(solution)/shard_map/reduce_scatter | solution.py:57
  49.7 2.4 %fusion.11 = f32[64,4096]{1,0:T(8,128)} fusion(f32[64,64]{1,0:T(8,128)} %reduce-scatter.8.cloned.1.call-done, bf16[1,64,4096]{2,1,0:T(8,128)(2,1)S(1)} %copy-done), kind=kOutput, calls=%fused_computation.18 | convolution fusion | flops 201326592 | bytes 1589248 | tf_op jit(solution)/shard_map/dot_general | solution.py:67
  52.1 0.0 all-reduce.5.cloned.1.call-update
  52.1 0.0 reduce-scatter.4.cloned.1.call-start
  52.2 11.4 %convolution_add_fusion = f32[256,4096]{1,0:T(8,128)} fusion(f32[256,4096]{1,0:T(8,128)} %fusion.15, bf16[1792,256]{1,0:T(8,128)(2,1)S(1)} %get-tuple-element.9, bf16[1792,4096]{1,0:T(8,128)(2,1)} %param.15), kind=kOutput, calls=%fused_computation | convolution fusion | flops 3759144960 | bytes 23986176 | tf_op jit(solution)/shard_map/dot_general | solution.py:83
  63.6 0.0 copy-start.1
  63.6 0.0 reduce-scatter.4.cloned.1.call-update
  63.6 0.0 copy-start.2
  63.6 0.0 all-reduce.7.cloned.1.call-start
  63.7 0.9 copy-done.1
  64.5 2.2 all_gather.12
  66.7 0.3 convolution_convert_fusion.1
  67.0 13.7 %all_gather.13 = bf16[256,64]{1,0:T(8,128)(2,1)S(1)} all-gather(bf16[64,64]{1,0:T(8,128)(2,1)S(1)} %convolution_convert_fusion.1), channel_id=1, replica_groups=mesh['groups'=2,'tensor'=4,'dp'=2,'pipe'=2] {'tensor'}, dimensions={0}, use_global_device_ids=true | all-gather | bytes 40960 | tf_op jit(solution)/shard_map/all_gather | solution.py:50
  80.7 0.0 copy-done.2
  80.7 2.2 all_gather.14
  82.9 0.3 convolution_convert_fusion
  83.2 14.2 %all_gather.15 = bf16[256,64]{1,0:T(8,128)(2,1)S(1)} all-gather(bf16[64,64]{1,0:T(8,128)(2,1)S(1)} %convolution_convert_fusion), channel_id=1, replica_groups=mesh['groups'=2,'tensor'=4,'dp'=2,'pipe'=2] {'tensor'}, dimensions={0}, use_global_device_ids=true | all-gather | bytes 40960 | tf_op jit(solution)/shard_map/all_gather | solution.py:51
  97.4 1.2 fusion.18
  98.6 1.2 fusion.19
  99.8 0.0 all-reduce.7.cloned.1.call-update
  99.8 78.0 %all-reduce.5.cloned.1.call-done = (f32[64,4096]{1,0:T(8,128)}, f32[64,4096]{1,0:T(8,128)}) async-done(((f32[64,4096]{1,0:T(8,128)}, f32[64,4096]{1,0:T(8,128)}), (f32[64,4096]{1,0:T(8,128)}, f32[64,4096]{1,0:T(8,128)})) %all-reduce.5.cloned.1.call-update) | async-done | bytes 2097168 | tf_op jit(solution)/shard_map/psum | solution.py:74
  177.8 2.3 constant_dynamic-slice_fusion
  180.0 0.0 reduce-scatter.4.cloned.1.call-done
  180.0 1.8 convert_bitcast_fusion
  181.8 36.6 %all-reduce.7.cloned.1.call-done = (f32[1792,64]{0,1:T(8,128)}, f32[1792,64]{0,1:T(8,128)}) async-done(((f32[1792,64]{0,1:T(8,128)}, f32[1792,64]{0,1:T(8,128)}), (f32[1792,64]{0,1:T(8,128)}, f32[1792,64]{0,1:T(8,128)})) %all-reduce.7.cloned.1.call-update) | async-done | bytes 917520 | tf_op jit(solution)/shard_map/psum | solution.py:79
  218.4 1.8 copy.19
  220.2 1.8 copy.20
Async XLA Ops:
  8.0 21.4 %copy-start = (bf16[1,64,4096]{2,1,0:T(8,128)(2,1)S(1)}, bf16[1,64,4096]{2,1,0:T(8,128)(2,1)}, u32[]{:S(2)}) copy-start(bf16[1,64,4096]{2,1,0:T(8,128)(2,1)} %param.10) | copy-start | bytes 1572868
  8.0 2.8 %copy-start.3 = (bf16[1792,64]{0,1:T(8,128)(2,1)S(1)}, bf16[1792,64]{0,1:T(8,128)(2,1)}, u32[]{:S(2)}) copy-start(bf16[1792,64]{0,1:T(8,128)(2,1)} %param.18) | copy-start | bytes 688132
  8.0 4.0 %copy-start.4 = (bf16[1792,64]{0,1:T(8,128)(2,1)S(1)}, bf16[1792,64]{0,1:T(8,128)(2,1)}, u32[]{:S(2)}) copy-start(bf16[1792,64]{0,1:T(8,128)(2,1)} %param.19) | copy-start | bytes 688132
  8.0 21.4 %reduce-scatter.6.cloned.1.call-start = ((), (), s32[]{:S(2)}) async-start(), calls=%async_computation.4 | async-start | bytes 163840 | tf_op jit(solution)/shard_map/reduce_scatter | solution.py:56
  12.0 37.8 %reduce-scatter.8.cloned.1.call-start = ((), (), s32[]{:S(2)}) async-start(), calls=%async_computation.5 | async-start | bytes 163840 | tf_op jit(solution)/shard_map/reduce_scatter | solution.py:57
  13.2 164.6 %all-reduce.5.cloned.1.call-start = ((), (), s32[]{:S(2)}) async-start(), calls=%async_computation.6 | async-start | bytes 4194304 | tf_op jit(solution)/shard_map/psum | solution.py:74
  52.1 127.9 %reduce-scatter.4.cloned.1.call-start = ((), (), s32[]{:S(2)}) async-start(), calls=%async_computation.3 | async-start | bytes 4718592 | tf_op jit(solution)/shard_map/reduce_scatter | solution.py:86
  63.6 1.0 copy-start.1
  63.6 17.1 %copy-start.2 = (bf16[64,2048]{1,0:T(8,128)(2,1)S(1)}, bf16[64,2048]{1,0:T(8,128)(2,1)}, u32[]{:S(2)}) copy-start(bf16[64,2048]{1,0:T(8,128)(2,1)} %param.17) | copy-start | bytes 786436
  63.6 154.8 %all-reduce.7.cloned.1.call-start = ((), (), s32[]{:S(2)}) async-start(), calls=%async_computation.7 | async-start | bytes 1835008 | tf_op jit(solution)/shard_map/psum | solution.py:79
Sparse Core Ops, SparseCore 0:
  12.1 17.3 reduce-scatter.5
  32.3 17.3 reduce-scatter.7
  53.3 124.3 all-reduce.4
  180.7 37.6 all-reduce.6
Sparse Core Ops, SparseCore 1:
  63.7 58.7 reduce-scatter.3
where the time goes:
time: 231 us; the launch traced here: 229 us
  waiting for transfers between devices  138 us (60%)
  blocking collectives  32.3 us (14%)
  matrix products  32 us (14%)
  between operations  15.3 us (7%)
  local copies, waits for them, and re-layouts  6.79 us (3%)
  other arithmetic  4.52 us (2%)
    psum x1, waiting for transfers between devices, body(): lax.psum((gate_a_part, up_a_part), ('tensor', 'dp', 'pipe'))  78 us
    psum x1, waiting for transfers between devices, body(): gate_b_grad, up_b_grad = lax.psum((gate_b_part, up_b_part), 'dp')  36.6 us
    reduce_scatter x1, waiting for transfers between devices, body(): lax.psum_scatter(up_backward, 'tensor', scatter_dimension=0, tiled=True)  17.9 us
    all_gather x1, blocking collectives, body(): lax.all_gather(own_up, 'tensor', axis=0, tiled=True)  14.2 us
    all_gather x1, blocking collectives, body(): lax.all_gather(own_gate, 'tensor', axis=0, tiled=True)  13.7 us
    dot_general x1, matrix products, body(): lax.dot_general(up_gradient, up_merged_weight, contract_leading, preferre...  11.4 us
    dot_general x1, matrix products, body(): lax.dot_general(gate_gradient, gate_merged_weight, contract_leading, pref...  10.7 us
    reduce_scatter x1, waiting for transfers between devices, body(): lax.psum_scatter(gate_backward, 'tensor', scatter_dimension=0, tiled=True)  5.51 us
  transfers between devices with their start and end apart: 5, of which 4 were waited for; matrix products, arithmetic and copies ran while one was open for 14% of the time, Pallas kernels for 0%

commit v1 on v0

v1 whole, which is shorter than its diff:
```python
import functools

import jax
import jax.numpy as jnp
from jax import lax
from jax.experimental import pallas as pl
from jax.experimental.pallas import tpu as pltpu
from jax.sharding import PartitionSpec as P

F32 = jnp.float32
BF16 = jnp.bfloat16
TILE = 512
SLOTS = 3


def remote(src, dst, send_sem, recv_sem, axis, index):
    return pltpu.make_async_remote_copy(
        src_ref=src,
        dst_ref=dst,
        send_sem=send_sem,
        recv_sem=recv_sem,
        device_id={axis: index},
        device_id_type=pl.DeviceIdType.MESH,
    )


def kernel(
    n,
    nd,
    tok,
    g,
    u,
    h,
    wg,
    wu,
    gd,
    ud,
    gu,
    uu,
    dx_out,
    ga_out,
    ua_out,
    gb_out,
    ub_out,
    grad_g,
    grad_u,
    trans_g,
    trans_u,
    wbuf,
    acc,
    pair_send,
    pair_recv,
    keep,
    z_send,
    z_recv,
    proj_pair,
    proj_all,
    back_pair,
    back_z,
    back_recv,
    b_all,
    ax_send,
    ax_recv,
    az_send,
    az_recv,
    a_all,
    w_sem,
    pair_ss,
    pair_rs,
    z_ss,
    z_rs,
    small_ss,
    small_rs,
    proj_ss,
    proj_rs,
    back_ss,
    back_rs,
    b_ss,
    b_rs,
    ax_ss,
    ax_rs,
    az_ss,
    az_rs,
    ag_ss,
    ag_rs,
    agx_ss,
    agx_rs,
):
    z = lax.axis_index("tensor")
    x = lax.axis_index("dp")
    c = lax.axis_index("pipe")
    other = 1 - c
    hidden, seq = g.shape
    width = wg.shape[1]
    tiles = width // TILE
    own = seq // (2 * n)
    half = gd.shape[1]
    rank = gd.shape[0]
    a_rows = 2 * rank // nd
    a_cols = half // n

    def weights(t, start):
        slot = lax.rem(t, SLOTS)
        columns = pl.ds(pl.multiple_of(t * TILE, TILE), TILE)
        for i, ref in enumerate((wg, wu)):
            copy = pltpu.make_async_copy(ref.at[:, columns], wbuf.at[slot, i], w_sem.at[slot, i])
            if start:
                copy.start()
            else:
                copy.wait()

    barrier = pltpu.get_barrier_semaphore()
    pl.semaphore_signal(
        barrier, inc=1, device_id={"pipe": other}, device_id_type=pl.DeviceIdType.MESH
    )
    for j in range(1, n):
        pl.semaphore_signal(
            barrier,
            inc=1,
            device_id={"tensor": lax.rem(z + j, n)},
            device_id_type=pl.DeviceIdType.MESH,
        )
    for j in range(1, nd):
        pl.semaphore_signal(
            barrier,
            inc=1,
            device_id={"dp": lax.rem(x + j, nd)},
            device_id_type=pl.DeviceIdType.MESH,
        )
    for t in range(SLOTS - 1):
        weights(t, True)

    tok_half = tok.at[:, pl.ds(pl.multiple_of(c * half, half), half)]
    down = jnp.concatenate([gd[...], ud[...]], axis=0)
    proj_pair[0] = lax.dot_general(
        tok_half[...], down, (((1,), (1,)), ((), ())), preferred_element_type=F32
    )
    pl.semaphore_wait(barrier, 1 + (n - 1) + (nd - 1))
    proj_copy = remote(
        proj_pair.at[0], proj_pair.at[1], small_ss.at[0], small_rs.at[0], "pipe", other
    )
    proj_copy.start()

    def activate(start, size):
        rows = pl.ds(start, size)
        gv = g[rows, :].astype(F32)
        uv = u[rows, :].astype(F32)
        hv = h[rows, :].astype(F32)
        s = jax.nn.sigmoid(gv)
        gg = (hv * uv * s * (1.0 + gv * (1.0 - s))).astype(BF16)
        ug = (hv * gv * s).astype(BF16)
        grad_g[rows, :] = gg
        grad_u[rows, :] = ug
        trans_g[:, rows] = gg.T
        trans_u[:, rows] = ug.T

    full = hidden // 128

    @pl.loop(0, full)
    def _(i):
        activate(pl.multiple_of(i * 128, 128), 128)

    if hidden % 128:
        activate(full * 128, hidden % 128)

    back_pair[0] = jnp.concatenate(
        [
            jnp.dot(trans_g[...], gu[...], preferred_element_type=F32),
            jnp.dot(trans_u[...], uu[...], preferred_element_type=F32),
        ],
        axis=1,
    )
    back_copy = remote(
        back_pair.at[0], back_pair.at[1], small_ss.at[1], small_rs.at[1], "pipe", other
    )
    back_copy.start()

    proj_copy.wait_recv()
    proj_all[z] = (proj_pair[0] + proj_pair[1]).astype(BF16)

    def proj_z(j):
        return remote(
            proj_all.at[z],
            proj_all.at[z],
            proj_ss.at[j - 1],
            proj_rs.at[j - 1],
            "tensor",
            lax.rem(z + j, n),
        )

    for j in range(1, n):
        proj_z(j).start()

    back_copy.wait_recv()
    back_z[...] = (back_pair[0] + back_pair[1]).reshape(back_z.shape)

    def back_to(j):
        to = lax.rem(z + j, n)
        return remote(
            back_z.at[to],
            back_recv.at[j - 1],
            back_ss.at[j - 1],
            back_rs.at[j - 1],
            "tensor",
            to,
        )

    for j in range(1, n):
        back_to(j).start()

    def b_to(j):
        return remote(
            b_all.at[x], b_all.at[x], b_ss.at[j - 1], b_rs.at[j - 1], "dp", lax.rem(x + j, nd)
        )

    def ax_to(j):
        to = lax.rem(x + j, nd)
        return remote(
            ax_send.at[to], ax_recv.at[j - 1], ax_ss.at[j - 1], ax_rs.at[j - 1], "dp", to
        )

    def az_to(j):
        to = lax.rem(z + j, n)
        return remote(
            az_send.at[to], az_recv.at[j - 1], az_ss.at[j - 1], az_rs.at[j - 1], "tensor", to
        )

    def ag_to(j):
        return remote(
            a_all.at[x, z],
            a_all.at[x, z],
            ag_ss.at[j - 1],
            ag_rs.at[j - 1],
            "tensor",
            lax.rem(z + j, n),
        )

    def agx_to(j):
        return remote(
            a_all.at[x], a_all.at[x], agx_ss.at[j - 1], agx_rs.at[j - 1], "dp", lax.rem(x + j, nd)
        )

    def a_partial():
        for j in range(1, n):
            back_to(j).wait_recv()
        total = back_z[z]
        for j in range(1, n):
            total = total + back_recv[j - 1]
        total = total.T
        high = total.astype(BF16)
        low = (total - high.astype(F32)).astype(BF16)
        part = jnp.dot(high, tok_half[...], preferred_element_type=F32)
        part = part + jnp.dot(low, tok_half[...], preferred_element_type=F32)
        for d in range(nd):
            ax_send[d] = part[d * a_rows : (d + 1) * a_rows].astype(BF16)
        for j in range(1, nd):
            ax_to(j).start()

    def b_partial():
        for j in range(1, n):
            proj_z(j).wait_recv()
        proj = proj_all[...].reshape(seq, 2 * rank)
        first = lax.broadcasted_iota(jnp.int32, proj.shape, 1) < rank
        zero = jnp.zeros_like(proj)
        part = jnp.dot(grad_g[...], jnp.where(first, proj, zero), preferred_element_type=F32)
        part = part + jnp.dot(grad_u[...], jnp.where(first, zero, proj), preferred_element_type=F32)
        b_all[x] = part.astype(BF16)
        for j in range(1, nd):
            b_to(j).start()

    def a_across():
        total = ax_send[x].astype(F32)
        for j in range(1, nd):
            ax_to(j).wait_recv()
        for j in range(1, nd):
            total = total + ax_recv[j - 1].astype(F32)
        for k in range(n):
            az_send[k] = total[:, k * a_cols : (k + 1) * a_cols].astype(BF16)
        for j in range(1, n):
            az_to(j).start()

    def a_along():
        total = az_send[z].astype(F32)
        for j in range(1, n):
            az_to(j).wait_recv()
        for j in range(1, n):
            total = total + az_recv[j - 1].astype(F32)
        a_all[x, z] = total.astype(BF16)
        for j in range(1, n):
            ag_to(j).start()

    def pair(t):
        return remote(
            pair_send.at[t], pair_recv.at[t], pair_ss.at[t], pair_rs.at[t], "pipe", other
        )

    def z_to(t, j):
        to = lax.rem(z + j, n)
        return remote(
            z_send.at[t, to], z_recv.at[t, j - 1], z_ss.at[t, j - 1], z_rs.at[t, j - 1], "tensor", to
        )

    def rows_of(k, core):
        return pl.ds(pl.multiple_of((2 * k + core) * own, own), own)

    def forward(t):
        slot = lax.rem(t, 2)
        pair(t).wait_recv()
        for k in range(n):
            z_send[t, k] = (acc[slot, rows_of(k, c), :] + pair_recv[t, k].astype(F32)).astype(BF16)
        for j in range(1, n):
            z_to(t, j).start()
        keep[t] = acc[slot, rows_of(z, c), :] + pair_recv[t, z].astype(F32)

    @pl.loop(0, tiles)
    def _(t):
        @pl.when(t + SLOTS - 1 < tiles)
        def _():
            weights(t + SLOTS - 1, True)

        weights(t, False)
        slot = lax.rem(t, 2)
        wslot = lax.rem(t, SLOTS)
        acc[slot] = jnp.dot(trans_g[...], wbuf[wslot, 0], preferred_element_type=F32) + jnp.dot(
            trans_u[...], wbuf[wslot, 1], preferred_element_type=F32
        )
        for k in range(n):
            pair_send[t, k] = acc[slot, rows_of(k, other), :].astype(BF16)
        pair(t).start()

        @pl.when(t > 0)
        def _():
            forward(t - 1)

        @pl.when(t == 1)
        def _():
            a_partial()

        @pl.when(t == 2)
        def _():
            b_partial()

        @pl.when(t == 4)
        def _():
            a_across()

        @pl.when(t == 6)
        def _():
            a_along()

    forward(tiles - 1)

    for j in range(1, n):
        ag_to(j).wait_recv()
    for j in range(1, nd):
        agx_to(j).start()

    for j in range(1, nd):
        b_to(j).wait_recv()
    total = b_all[0].astype(F32)
    for d in range(1, nd):
        total = total + b_all[d].astype(F32)
    gb_out[...] = total[:, :rank]
    ub_out[...] = total[:, rank:]

    @pl.loop(0, tiles)
    def _(t):
        total = keep[t]
        for j in range(1, n):
            z_to(t, j).wait_recv()
        for j in range(1, n):
            total = total + z_recv[t, j - 1].astype(F32)
        dx_out[:, pl.ds(pl.multiple_of(t * TILE, TILE), TILE)] = total.astype(BF16)
        pair(t).wait_send()
        for j in range(1, n):
            z_to(t, j).wait_send()

    for j in range(1, nd):
        agx_to(j).wait_recv()
    for d in range(nd):
        first = d * a_rows
        ref, row = (ga_out, first) if first < rank else (ua_out, first - rank)
        for k in range(n):
            ref[row : row + a_rows, k * a_cols : (k + 1) * a_cols] = a_all[d, k].astype(F32)

    proj_copy.wait_send()
    back_copy.wait_send()
    for j in range(1, n):
        proj_z(j).wait_send()
        back_to(j).wait_send()
        az_to(j).wait_send()
        ag_to(j).wait_send()
    for j in range(1, nd):
        b_to(j).wait_send()
        ax_to(j).wait_send()
        agx_to(j).wait_send()


def body(n, nd, tokens, gate, up, hidden_gradient, wg, wu, gd, ud, gu, uu):
    hidden, seq = gate.shape[1:]
    rows, width = tokens.shape[1:]
    rank, half = gd.shape
    tiles = width // TILE
    own = seq // (2 * n)
    a_rows = 2 * rank // nd
    a_cols = half // n
    dma = pltpu.SemaphoreType.DMA
    vmem = pl.BlockSpec(memory_space=pltpu.VMEM)
    hbm = pl.BlockSpec(memory_space=pl.ANY)
    outs = pl.pallas_call(
        functools.partial(kernel, n, nd),
        out_shape=(
            jax.ShapeDtypeStruct((own, width), BF16),
            jax.ShapeDtypeStruct((rank, half), F32),
            jax.ShapeDtypeStruct((rank, half), F32),
            jax.ShapeDtypeStruct((hidden, rank), F32),
            jax.ShapeDtypeStruct((hidden, rank), F32),
        ),
        in_specs=[vmem] * 4 + [hbm] * 2 + [vmem] * 4,
        out_specs=(vmem,) * 5,
        scratch_shapes=[
            pltpu.VMEM((hidden, seq), BF16),
            pltpu.VMEM((hidden, seq), BF16),
            pltpu.VMEM((seq, hidden), BF16),
            pltpu.VMEM((seq, hidden), BF16),
            pltpu.VMEM((SLOTS, 2, hidden, TILE), BF16),
            pltpu.VMEM((2, seq, TILE), F32),
            pltpu.VMEM((tiles, n, own, TILE), BF16),
            pltpu.VMEM((tiles, n, own, TILE), BF16),
            pltpu.VMEM((tiles, own, TILE), F32),
            pltpu.VMEM((tiles, n, own, TILE), BF16),
            pltpu.VMEM((tiles, n - 1, own, TILE), BF16),
            pltpu.VMEM((2, rows, 2 * rank), F32),
            pltpu.VMEM((n, rows, 2 * rank), BF16),
            pltpu.VMEM((2, seq, 2 * rank), F32),
            pltpu.VMEM((n, rows, 2 * rank), F32),
            pltpu.VMEM((n - 1, rows, 2 * rank), F32),
            pltpu.VMEM((nd, hidden, 2 * rank), BF16),
            pltpu.VMEM((nd, a_rows, half), BF16),
            pltpu.VMEM((nd - 1, a_rows, half), BF16),
            pltpu.VMEM((n, a_rows, a_cols), BF16),
            pltpu.VMEM((n - 1, a_rows, a_cols), BF16),
            pltpu.VMEM((nd, n, a_rows, a_cols), BF16),
            dma((SLOTS, 2)),
            dma((tiles,)),
            dma((tiles,)),
            dma((tiles, n - 1)),
            dma((tiles, n - 1)),
            dma((2,)),
            dma((2,)),
            dma((n - 1,)),
            dma((n - 1,)),
            dma((n - 1,)),
            dma((n - 1,)),
            dma((nd - 1,)),
            dma((nd - 1,)),
            dma((nd - 1,)),
            dma((nd - 1,)),
            dma((n - 1,)),
            dma((n - 1,)),
            dma((n - 1,)),
            dma((n - 1,)),
            dma((nd - 1,)),
            dma((nd - 1,)),
        ],
        compiler_params=pltpu.CompilerParams(
            collective_id=0, has_side_effects=True, vmem_limit_bytes=56 * 1024 * 1024
        ),
        cost_estimate=pl.CostEstimate(
            flops=4 * seq * hidden * width, bytes_accessed=4 * hidden * width, transcendentals=0
        ),
    )(tokens[0], gate[0], up[0], hidden_gradient[0], wg, wu, gd, ud, gu, uu)
    return (outs[0][None],) + tuple(outs[1:])


def solution(mesh):
    placed = (
        P(("groups", "dp"), "tensor", None),
        P(("groups", "dp"), ("tensor", "pipe"), None),
        P(("groups", "dp"), ("tensor", "pipe"), None),
        P(("groups", "dp"), ("tensor", "pipe"), None),
        P(("tensor", "pipe"), None),
        P(("tensor", "pipe"), None),
        P(None, "pipe"),
        P(None, "pipe"),
        P(("tensor", "pipe"), None),
        P(("tensor", "pipe"), None),
    )
    return jax.shard_map(
        functools.partial(body, mesh.shape["tensor"], mesh.shape["dp"]),
        mesh=mesh,
        in_specs=placed,
        out_specs=(
            P(("groups", "dp"), ("tensor", "pipe"), None),
            P("groups", "pipe"),
            P("groups", "pipe"),
            P(("groups", "tensor", "pipe"), None),
            P(("groups", "tensor", "pipe"), None),
        ),
        check_vma=False,
    )
```

time: 231 us -> 70.4 us (0.30)
  waiting for transfers between devices: 138 us -> 0 us
  Pallas kernels: 0 us -> 55.6 us
  blocking collectives: 32.3 us -> 0 us
  matrix products: 32 us -> 0 us
  between operations: 15.3 us -> 0.64 us
  local copies, waits for them, and re-layouts: 6.79 us -> 13.7 us
  other arithmetic: 4.52 us -> 0 us
    psum x2 -> x0, waiting for transfers between devices: 115 us -> none  [the longest x1 78 us: body(): lax.psum((gate_a_part, up_a_part), ('tensor', 'dp', 'pipe'))]
    pallas_call x0 -> x1, Pallas kernels: none -> 55.6 us  [body(): pl.pallas_call(functools.partial(kernel, n, nd), out_shape=(jax.ShapeDtyp...]
    all_gather x4 -> x0, blocking collectives: 32.3 us -> none  [the longest x1 14.2 us: body(): lax.all_gather(own_up, 'tensor', axis=0, tiled=True)]
    dot_general x10 -> x0, matrix products: 32 us -> none  [the longest x1 11.4 us: body(): lax.dot_general(up_gradient, up_merged_weight, contract_leading, preferre...]
    reduce_scatter x3 -> x0, waiting for transfers between devices: 23.5 us -> none  [the longest x1 17.9 us: body(): lax.psum_scatter(up_backward, 'tensor', scatter_dimension=0, tiled=True)]
    unnamed x12 -> x7, local copies, waits for them, and re-layouts: 4.52 us -> 13.7 us
    convert_element_type x1 -> x0, other arithmetic: 2.75 us -> none  [body(): up_gradient = (grad_vals * gate_vals * sigmoid).astype(jnp.bfloat16)]
  transfers between devices with their start and end apart: 5 -> 0, of which waited for: 4 -> 0; matrix products, arithmetic and copies ran while one was open for 14% -> 0% of each run, Pallas kernels for 0% -> 0%
where the time goes in v1:
time: 70.4 us; the launch traced here: 70 us
  Pallas kernels  55.6 us (79%)
  local copies, waits for them, and re-layouts  13.7 us (19%)
    pallas_call x1, Pallas kernels, body(): pl.pallas_call(functools.partial(kernel, n, nd), out_shape=(jax.ShapeDtyp...  55.6 us
    unnamed x7, local copies, waits for them, and re-layouts  13.7 us

profile of v1, /device:TPU:28, one launch (start us, length us, event | category | flops | bytes accessed | tf_op | source)
XLA Modules:
  0.0 70.0 jit_solution(10850662038415389929)
XLA Ops:
  0.6 1.9 %copy.15.gu = bf16[1792,64]{1,0:T(8,128)(2,1)} copy(bf16[1792,64]{0,1:T(8,128)(2,1)} %param.18) | data formatting | bytes 458752 | tf_op args[8]
  2.5 1.9 %copy.16.uu = bf16[1792,64]{1,0:T(8,128)(2,1)} copy(bf16[1792,64]{0,1:T(8,128)(2,1)} %param.19) | data formatting | bytes 458752 | tf_op args[9]
  4.5 55.6 %shard_map.137 = (bf16[32,4096]{1,0:T(8,128)(2,1)}, f32[64,2048]{1,0:T(8,128)}, f32[64,2048]{1,0:T(8,128)}, f32[1792,64]{1,0:T(8,128)}, f32[1792,64]{1,0:T(8,128)}) custom-call(bf16[64,4096]{1,0:T(8,128)(2,1)} %bitcast.8, bf16[1792,256]{1,0:T(8,128)(2,1)} %bitcast.5, bf16[1792,256]{1,0:T(8,128)(2,1)} %bitcast.6, bf16[1792,256]{1,0:T(8,128)(2,1)} %bitcast.7, ...), custom_call_target="tpu_custom_call" | custom-call | flops 7516192768 | bytes 29360128 | tf_op jit(solution)/shard_map/pallas_call | solution.py:410
  60.1 2.2 %copy.17 = f32[1792,64]{0,1:T(8,128)} copy(f32[1792,64]{1,0:T(8,128)} %get-tuple-element.18) | data formatting | bytes 917504
  62.3 2.2 %copy.18 = f32[1792,64]{0,1:T(8,128)} copy(f32[1792,64]{1,0:T(8,128)} %get-tuple-element.19) | data formatting | bytes 917504
  64.6 1.7 %copy.22 = bf16[1,32,4096]{2,1,0:T(8,128)(2,1)} copy(bf16[1,32,4096]{2,1,0:T(8,128)(2,1)} %bitcast.9) | data formatting | bytes 524288
  66.2 1.9 %copy.23 = f32[64,2048]{1,0:T(8,128)} copy(f32[64,2048]{1,0:T(8,128)} %get-tuple-element.26) | data formatting | bytes 1048576
  68.1 1.9 %copy.24 = f32[64,2048]{1,0:T(8,128)} copy(f32[64,2048]{1,0:T(8,128)} %get-tuple-element.27) | data formatting | bytes 1048576

commit v2 on v1

--- a/solution.py
+++ b/solution.py
@@ -28,9 +28,9 @@
     n,
     nd,
     tok,
-    g,
-    u,
-    h,
+    g_hbm,
+    u_hbm,
+    h_hbm,
     wg,
     wu,
     gd,
@@ -38,12 +38,11 @@
     gu,
     uu,
     dx_out,
-    ga_out,
-    ua_out,
-    gb_out,
-    ub_out,
-    grad_g,
-    grad_u,
+    a_out,
+    b_out,
+    g,
+    u,
+    h,
     trans_g,
     trans_u,
     wbuf,
@@ -85,6 +84,8 @@
     ag_rs,
     agx_ss,
     agx_rs,
+    in_sem,
+    out_sem,
 ):
     z = lax.axis_index("tensor")
     x = lax.axis_index("dp")
@@ -127,6 +128,12 @@
             device_id={"dp": lax.rem(x + j, nd)},
             device_id_type=pl.DeviceIdType.MESH,
         )
+    loads = [
+        pltpu.make_async_copy(src, dst, in_sem.at[i])
+        for i, (src, dst) in enumerate(((g_hbm, g), (u_hbm, u), (h_hbm, h)))
+    ]
+    for load in loads:
+        load.start()
     for t in range(SLOTS - 1):
         weights(t, True)
 
@@ -149,11 +156,11 @@
         s = jax.nn.sigmoid(gv)
         gg = (hv * uv * s * (1.0 + gv * (1.0 - s))).astype(BF16)
         ug = (hv * gv * s).astype(BF16)
-        grad_g[rows, :] = gg
-        grad_u[rows, :] = ug
         trans_g[:, rows] = gg.T
         trans_u[:, rows] = ug.T
 
+    for load in loads:
+        load.wait()
     full = hidden // 128
 
     @pl.loop(0, full)
@@ -165,8 +172,12 @@
 
     back_pair[0] = jnp.concatenate(
         [
-            jnp.dot(trans_g[...], gu[...], preferred_element_type=F32),
-            jnp.dot(trans_u[...], uu[...], preferred_element_type=F32),
+            lax.dot_general(
+                trans_g[...], gu[...], (((1,), (1,)), ((), ())), preferred_element_type=F32
+            ),
+            lax.dot_general(
+                trans_u[...], uu[...], (((1,), (1,)), ((), ())), preferred_element_type=F32
+            ),
         ],
         axis=1,
     )
@@ -259,12 +270,12 @@
     def b_partial():
         for j in range(1, n):
             proj_z(j).wait_recv()
-        proj = proj_all[...].reshape(seq, 2 * rank)
-        first = lax.broadcasted_iota(jnp.int32, proj.shape, 1) < rank
-        zero = jnp.zeros_like(proj)
-        part = jnp.dot(grad_g[...], jnp.where(first, proj, zero), preferred_element_type=F32)
-        part = part + jnp.dot(grad_u[...], jnp.where(first, zero, proj), preferred_element_type=F32)
-        b_all[x] = part.astype(BF16)
+        proj = proj_all[...].reshape(seq, 2 * rank).T
+        for i, ref in enumerate((trans_g, trans_u)):
+            rows = slice(i * rank, (i + 1) * rank)
+            b_all[x, rows, :] = jnp.dot(
+                proj[rows], ref[...], preferred_element_type=F32
+            ).astype(BF16)
         for j in range(1, nd):
             b_to(j).start()
 
@@ -332,19 +343,19 @@
         def _():
             forward(t - 1)
 
+        @pl.when(t == 0)
+        def _():
+            a_partial()
+
         @pl.when(t == 1)
         def _():
-            a_partial()
-
-        @pl.when(t == 2)
-        def _():
             b_partial()
 
-        @pl.when(t == 4)
+        @pl.when(t == 3)
         def _():
             a_across()
 
-        @pl.when(t == 6)
+        @pl.when(t == 5)
         def _():
             a_along()
 
@@ -357,11 +368,8 @@
 
     for j in range(1, nd):
         b_to(j).wait_recv()
-    total = b_all[0].astype(F32)
-    for d in range(1, nd):
-        total = total + b_all[d].astype(F32)
-    gb_out[...] = total[:, :rank]
-    ub_out[...] = total[:, rank:]
+    b_store = pltpu.make_async_copy(b_all, b_out, out_sem.at[0])
+    b_store.start()
 
     @pl.loop(0, tiles)
     def _(t):
@@ -377,11 +385,10 @@
 
     for j in range(1, nd):
         agx_to(j).wait_recv()
-    for d in range(nd):
-        first = d * a_rows
-        ref, row = (ga_out, first) if first < rank else (ua_out, first - rank)
-        for k in range(n):
-            ref[row : row + a_rows, k * a_cols : (k + 1) * a_cols] = a_all[d, k].astype(F32)
+    a_store = pltpu.make_async_copy(a_all, a_out, out_sem.at[1])
+    a_store.start()
+    a_store.wait()
+    b_store.wait()
 
     proj_copy.wait_send()
     back_copy.wait_send()
@@ -394,6 +401,23 @@
         b_to(j).wait_send()
         ax_to(j).wait_send()
         agx_to(j).wait_send()
+
+
+def finish(dx, a_all, b_all, dx_out, ga_out, ua_out, gb_out, ub_out):
+    nd, n, a_rows, a_cols = a_all.shape
+    rank = ga_out.shape[0]
+    dx_out[...] = dx[...]
+    for d in range(nd):
+        first = d * a_rows
+        ref, row = (ga_out, first) if first < rank else (ua_out, first - rank)
+        for k in range(n):
+            ref[row : row + a_rows, k * a_cols : (k + 1) * a_cols] = a_all[d, k].astype(F32)
+    for i, ref in enumerate((gb_out, ub_out)):
+        rows = slice(i * rank, (i + 1) * rank)
+        total = b_all[0, rows, :].astype(F32)
+        for d in range(1, nd):
+            total = total + b_all[d, rows, :].astype(F32)
+        ref[...] = total
 
 
 def body(n, nd, tokens, gate, up, hidden_gradient, wg, wu, gd, ud, gu, uu):
@@ -411,14 +435,13 @@
         functools.partial(kernel, n, nd),
         out_shape=(
             jax.ShapeDtypeStruct((own, width), BF16),
-            jax.ShapeDtypeStruct((rank, half), F32),
-            jax.ShapeDtypeStruct((rank, half), F32),
-            jax.ShapeDtypeStruct((hidden, rank), F32),
-            jax.ShapeDtypeStruct((hidden, rank), F32),
+            jax.ShapeDtypeStruct((nd, n, a_rows, a_cols), BF16),
+            jax.ShapeDtypeStruct((nd, 2 * rank, hidden), BF16),
         ),
-        in_specs=[vmem] * 4 + [hbm] * 2 + [vmem] * 4,
-        out_specs=(vmem,) * 5,
+        in_specs=[vmem] + [hbm] * 5 + [vmem] * 4,
+        out_specs=(vmem, hbm, hbm),
         scratch_shapes=[
+            pltpu.VMEM((hidden, seq), BF16),
             pltpu.VMEM((hidden, seq), BF16),
             pltpu.VMEM((hidden, seq), BF16),
             pltpu.VMEM((seq, hidden), BF16),
@@ -435,7 +458,7 @@
             pltpu.VMEM((2, seq, 2 * rank), F32),
             pltpu.VMEM((n, rows, 2 * rank), F32),
             pltpu.VMEM((n - 1, rows, 2 * rank), F32),
-            pltpu.VMEM((nd, hidden, 2 * rank), BF16),
+            pltpu.VMEM((nd, 2 * rank, hidden), BF16),
             pltpu.VMEM((nd, a_rows, half), BF16),
             pltpu.VMEM((nd - 1, a_rows, half), BF16),
             pltpu.VMEM((n, a_rows, a_cols), BF16),
@@ -462,6 +485,8 @@
             dma((n - 1,)),
             dma((nd - 1,)),
             dma((nd - 1,)),
+            dma((3,)),
+            dma((2,)),
         ],
         compiler_params=pltpu.CompilerParams(
             collective_id=0, has_side_effects=True, vmem_limit_bytes=56 * 1024 * 1024
@@ -469,8 +494,21 @@
         cost_estimate=pl.CostEstimate(
             flops=4 * seq * hidden * width, bytes_accessed=4 * hidden * width, transcendentals=0
         ),
-    )(tokens[0], gate[0], up[0], hidden_gradient[0], wg, wu, gd, ud, gu, uu)
-    return (outs[0][None],) + tuple(outs[1:])
+    )(tokens[0], gate[0], up[0], hidden_gradient[0], wg, wu, gd, ud, gu.T, uu.T)
+    dx, ga, ua, gb, ub = pl.pallas_call(
+        finish,
+        out_shape=(
+            jax.ShapeDtypeStruct((own, width), BF16),
+            jax.ShapeDtypeStruct((rank, half), F32),
+            jax.ShapeDtypeStruct((rank, half), F32),
+            jax.ShapeDtypeStruct((rank, hidden), F32),
+            jax.ShapeDtypeStruct((rank, hidden), F32),
+        ),
+        in_specs=[vmem] * 3,
+        out_specs=(vmem,) * 5,
+        compiler_params=pltpu.CompilerParams(vmem_limit_bytes=32 * 1024 * 1024),
+    )(*outs)
+    return dx[None], ga, ua, gb.T, ub.T
 
 
 def solution(mesh):

time: 70.4 us -> 62.4 us (0.89)
  local copies, waits for them, and re-layouts: 13.7 us -> 3.16 us
  Pallas kernels: 55.6 us -> 58.4 us
    unnamed x7 -> x6, local copies, waits for them, and re-layouts: 13.7 us -> 3.16 us
    pallas_call x0 -> x1, Pallas kernels: none -> 1.45 us  [body(): pl.pallas_call(finish, out_shape=(jax.ShapeDtypeStruct((own, width), BF16...]
    pallas_call x1, Pallas kernels: 55.6 us -> 56.9 us  [body(): pl.pallas_call(functools.partial(kernel, n, nd), out_shape=(jax.ShapeDtyp...]
where the time goes in v2:
time: 62.4 us; the launch traced here: 62.2 us
  Pallas kernels  58.4 us (94%)
  local copies, waits for them, and re-layouts  3.16 us (5%)
  between operations  0.65 us (1%)
    pallas_call x1, Pallas kernels, body(): pl.pallas_call(functools.partial(kernel, n, nd), out_shape=(jax.ShapeDtyp...  56.9 us
    unnamed x6, local copies, waits for them, and re-layouts  3.16 us
    pallas_call x1, Pallas kernels, body(): pl.pallas_call(finish, out_shape=(jax.ShapeDtypeStruct((own, width), BF16...  1.45 us

profile of v2, /device:TPU:28, one launch (start us, length us, event | category | flops | bytes accessed | tf_op | source)
XLA Modules:
  0.0 62.2 jit_solution(4339823422849856411)
XLA Ops:
  0.6 56.9 %shard_map.137 = (bf16[32,4096]{1,0:T(8,128)(2,1)}, bf16[2,4,64,512]{3,2,1,0:T(8,128)(2,1)}, bf16[2,128,1792]{2,1,0:T(8,128)(2,1)}) custom-call(bf16[64,4096]{1,0:T(8,128)(2,1)} %bitcast.12, bf16[1792,256]{1,0:T(8,128)(2,1)} %bitcast.9, bf16[1792,256]{1,0:T(8,128)(2,1)} %bitcast.10, bf16[1792,256]{1,0:T(8,128)(2,1)} %bitcast.11, bf16[1792,4096]{1,0:T(8,128)(2,1)} %wg.1, ...), custom_call_target="tpu_custom_call" | custom-call | flops 7516192768 | bytes 29360128 | tf_op jit(solution)/shard_map/pallas_call | solution.py:434
  57.6 0.0 copy-start
  57.6 1.2 %copy-done = bf16[2,128,1792]{2,1,0:T(8,128)(2,1)S(1)} copy-done((bf16[2,128,1792]{2,1,0:T(8,128)(2,1)S(1)}, bf16[2,128,1792]{2,1,0:T(8,128)(2,1)}, u32[]{:S(2)}) %copy-start) | copy-done | bytes 917528
  58.7 0.0 copy-start.1
  58.7 1.0 %copy-done.1 = bf16[2,4,64,512]{3,2,1,0:T(8,128)(2,1)S(1)} copy-done((bf16[2,4,64,512]{3,2,1,0:T(8,128)(2,1)S(1)}, bf16[2,4,64,512]{3,2,1,0:T(8,128)(2,1)}, u32[]{:S(2)}) %copy-start.1) | copy-done | bytes 524312
  59.8 0.0 copy-start.2
  59.8 0.9 %copy-done.2 = bf16[32,4096]{1,0:T(8,128)(2,1)S(1)} copy-done((bf16[32,4096]{1,0:T(8,128)(2,1)S(1)}, bf16[32,4096]{1,0:T(8,128)(2,1)}, u32[]{:S(2)}) %copy-start.2) | copy-done | bytes 262168
  60.7 1.5 %shard_map.138 = (bf16[32,4096]{1,0:T(8,128)(2,1)}, f32[64,2048]{1,0:T(8,128)}, f32[64,2048]{1,0:T(8,128)}, f32[64,1792]{1,0:T(8,128)}, f32[64,1792]{1,0:T(8,128)}) custom-call(bf16[32,4096]{1,0:T(8,128)(2,1)S(1)} %copy-done.2, bf16[2,4,64,512]{3,2,1,0:T(8,128)(2,1)S(1)} %copy-done.1, bf16[2,128,1792]{2,1,0:T(8,128)(2,1)S(1)} %copy-done), custom_call_target="tpu_custom_call" | custom-call | tf_op jit(solution)/shard_map/pallas_call | solution.py:498
Async XLA Ops:
  57.6 1.2 %copy-start = (bf16[2,128,1792]{2,1,0:T(8,128)(2,1)S(1)}, bf16[2,128,1792]{2,1,0:T(8,128)(2,1)}, u32[]{:S(2)}) copy-start(bf16[2,128,1792]{2,1,0:T(8,128)(2,1)} %get-tuple-element.15.b_all) | copy-start | bytes 2752516
  58.7 1.0 %copy-start.1 = (bf16[2,4,64,512]{3,2,1,0:T(8,128)(2,1)S(1)}, bf16[2,4,64,512]{3,2,1,0:T(8,128)(2,1)}, u32[]{:S(2)}) copy-start(bf16[2,4,64,512]{3,2,1,0:T(8,128)(2,1)} %get-tuple-element.14.a_all) | copy-start | bytes 1572868
  59.8 0.9 %copy-start.2 = (bf16[32,4096]{1,0:T(8,128)(2,1)S(1)}, bf16[32,4096]{1,0:T(8,128)(2,1)}, u32[]{:S(2)}) copy-start(bf16[32,4096]{1,0:T(8,128)(2,1)} %get-tuple-element.13.dx) | copy-start | bytes 786436

commit v3 on v2

--- a/solution.py
+++ b/solution.py
@@ -49,9 +49,10 @@
     acc,
     pair_send,
     pair_recv,
-    keep,
+    sums,
     z_send,
-    z_recv,
+    from_below,
+    from_above,
     proj_pair,
     proj_all,
     back_pair,
@@ -67,7 +68,8 @@
     pair_ss,
     pair_rs,
     z_ss,
-    z_rs,
+    below_rs,
+    above_rs,
     small_ss,
     small_rs,
     proj_ss,
@@ -305,11 +307,47 @@
             pair_send.at[t], pair_recv.at[t], pair_ss.at[t], pair_rs.at[t], "pipe", other
         )
 
-    def z_to(t, j):
-        to = lax.rem(z + j, n)
-        return remote(
-            z_send.at[t, to], z_recv.at[t, j - 1], z_ss.at[t, j - 1], z_rs.at[t, j - 1], "tensor", to
-        )
+    def up_to(t, k):
+        return remote(
+            z_send.at[t, k], from_below.at[t, k], z_ss.at[t, k], below_rs.at[t, k], "tensor", lax.rem(z + 1, n)
+        )
+
+    def down_to(t, k):
+        return remote(
+            z_send.at[t, k], from_above.at[t, k], z_ss.at[t, k], above_rs.at[t, k], "tensor", lax.rem(z + n - 1, n)
+        )
+
+    def climb(t):
+        for k in range(1, n):
+
+            @pl.when(k > z)
+            def _():
+                @pl.when(z > 0)
+                def _():
+                    up_to(t, k).wait_recv()
+                    z_send[t, k] = (sums[t, k] + from_below[t, k].astype(F32)).astype(BF16)
+
+                @pl.when(z == 0)
+                def _():
+                    z_send[t, k] = sums[t, k].astype(BF16)
+
+                up_to(t, k).start()
+
+    def descend(t):
+        for k in range(n - 1):
+
+            @pl.when(k < z)
+            def _():
+                @pl.when(z < n - 1)
+                def _():
+                    down_to(t, k).wait_recv()
+                    z_send[t, k] = (sums[t, k] + from_above[t, k].astype(F32)).astype(BF16)
+
+                @pl.when(z == n - 1)
+                def _():
+                    z_send[t, k] = sums[t, k].astype(BF16)
+
+                down_to(t, k).start()
 
     def rows_of(k, core):
         return pl.ds(pl.multiple_of((2 * k + core) * own, own), own)
@@ -318,13 +356,9 @@
         slot = lax.rem(t, 2)
         pair(t).wait_recv()
         for k in range(n):
-            z_send[t, k] = (acc[slot, rows_of(k, c), :] + pair_recv[t, k].astype(F32)).astype(BF16)
-        for j in range(1, n):
-            z_to(t, j).start()
-        keep[t] = acc[slot, rows_of(z, c), :] + pair_recv[t, z].astype(F32)
-
-    @pl.loop(0, tiles)
-    def _(t):
+            sums[t, k] = acc[slot, rows_of(k, c), :] + pair_recv[t, k].astype(F32)
+
+    def multiply(t):
         @pl.when(t + SLOTS - 1 < tiles)
         def _():
             weights(t + SLOTS - 1, True)
@@ -339,10 +373,27 @@
             pair_send[t, k] = acc[slot, rows_of(k, other), :].astype(BF16)
         pair(t).start()
 
-        @pl.when(t > 0)
+    @pl.loop(0, tiles + n - 1)
+    def _(t):
+        @pl.when(t < tiles)
+        def _():
+            multiply(t)
+
+        @pl.when((t > 0) & (t <= tiles))
         def _():
             forward(t - 1)
 
+        rising = t - 1 - z
+        falling = t - n + z
+
+        @pl.when((rising >= 0) & (rising < tiles))
+        def _():
+            climb(rising)
+
+        @pl.when((falling >= 0) & (falling < tiles))
+        def _():
+            descend(falling)
+
         @pl.when(t == 0)
         def _():
             a_partial()
@@ -358,8 +409,6 @@
         @pl.when(t == 5)
         def _():
             a_along()
-
-    forward(tiles - 1)
 
     for j in range(1, n):
         ag_to(j).wait_recv()
@@ -373,15 +422,23 @@
 
     @pl.loop(0, tiles)
     def _(t):
-        total = keep[t]
-        for j in range(1, n):
-            z_to(t, j).wait_recv()
-        for j in range(1, n):
-            total = total + z_recv[t, j - 1].astype(F32)
-        dx_out[:, pl.ds(pl.multiple_of(t * TILE, TILE), TILE)] = total.astype(BF16)
+        @pl.when(z > 0)
+        def _():
+            up_to(t, z).wait_recv()
+            sums[t, z] = sums[t, z] + from_below[t, z].astype(F32)
+
+        @pl.when(z < n - 1)
+        def _():
+            down_to(t, z).wait_recv()
+            sums[t, z] = sums[t, z] + from_above[t, z].astype(F32)
+
+        dx_out[:, pl.ds(pl.multiple_of(t * TILE, TILE), TILE)] = sums[t, z].astype(BF16)
         pair(t).wait_send()
-        for j in range(1, n):
-            z_to(t, j).wait_send()
+        for k in range(n):
+
+            @pl.when(k != z)
+            def _():
+                up_to(t, k).wait_send()
 
     for j in range(1, nd):
         agx_to(j).wait_recv()
@@ -450,9 +507,10 @@
             pltpu.VMEM((2, seq, TILE), F32),
             pltpu.VMEM((tiles, n, own, TILE), BF16),
             pltpu.VMEM((tiles, n, own, TILE), BF16),
-            pltpu.VMEM((tiles, own, TILE), F32),
+            pltpu.VMEM((tiles, n, own, TILE), F32),
             pltpu.VMEM((tiles, n, own, TILE), BF16),
-            pltpu.VMEM((tiles, n - 1, own, TILE), BF16),
+            pltpu.VMEM((tiles, n, own, TILE), BF16),
+            pltpu.VMEM((tiles, n, own, TILE), BF16),
             pltpu.VMEM((2, rows, 2 * rank), F32),
             pltpu.VMEM((n, rows, 2 * rank), BF16),
             pltpu.VMEM((2, seq, 2 * rank), F32),
@@ -467,8 +525,9 @@
             dma((SLOTS, 2)),
             dma((tiles,)),
             dma((tiles,)),
-            dma((tiles, n - 1)),
-            dma((tiles, n - 1)),
+            dma((tiles, n)),
+            dma((tiles, n)),
+            dma((tiles, n)),
             dma((2,)),
             dma((2,)),
             dma((n - 1,)),

time: 62.4 us -> 62.2 us (level)
  the two profiles are of different devices: /device:TPU:28 before, /device:TPU:8 now
where the time goes in v3:
time: 62.2 us; the launch traced here: 61.9 us
  Pallas kernels  58.1 us (93%)
  local copies, waits for them, and re-layouts  3.16 us (5%)
  between operations  0.65 us (1%)
    pallas_call x1, Pallas kernels, body(): pl.pallas_call(functools.partial(kernel, n, nd), out_shape=(jax.ShapeDtyp...  56.6 us
    unnamed x6, local copies, waits for them, and re-layouts  3.16 us
    pallas_call x1, Pallas kernels, body(): pl.pallas_call(finish, out_shape=(jax.ShapeDtypeStruct((own, width), BF16...  1.45 us

profile of v3, /device:TPU:8, one launch (start us, length us, event | category | flops | bytes accessed | tf_op | source)
XLA Modules:
  0.0 61.9 jit_solution(7411484965976663864)
XLA Ops:
  0.6 56.6 %shard_map.137 = (bf16[32,4096]{1,0:T(8,128)(2,1)}, bf16[2,4,64,512]{3,2,1,0:T(8,128)(2,1)}, bf16[2,128,1792]{2,1,0:T(8,128)(2,1)}) custom-call(bf16[64,4096]{1,0:T(8,128)(2,1)} %bitcast.12, bf16[1792,256]{1,0:T(8,128)(2,1)} %bitcast.9, bf16[1792,256]{1,0:T(8,128)(2,1)} %bitcast.10, bf16[1792,256]{1,0:T(8,128)(2,1)} %bitcast.11, bf16[1792,4096]{1,0:T(8,128)(2,1)} %wg.1, ...), custom_call_target="tpu_custom_call" | custom-call | flops 7516192768 | bytes 29360128 | tf_op jit(solution)/shard_map/pallas_call | solution.py:491
  57.3 0.0 copy-start
  57.3 1.2 %copy-done = bf16[2,128,1792]{2,1,0:T(8,128)(2,1)S(1)} copy-done((bf16[2,128,1792]{2,1,0:T(8,128)(2,1)S(1)}, bf16[2,128,1792]{2,1,0:T(8,128)(2,1)}, u32[]{:S(2)}) %copy-start) | copy-done | bytes 917528
  58.5 0.0 copy-start.1
  58.5 1.0 %copy-done.1 = bf16[2,4,64,512]{3,2,1,0:T(8,128)(2,1)S(1)} copy-done((bf16[2,4,64,512]{3,2,1,0:T(8,128)(2,1)S(1)}, bf16[2,4,64,512]{3,2,1,0:T(8,128)(2,1)}, u32[]{:S(2)}) %copy-start.1) | copy-done | bytes 524312
  59.5 0.0 copy-start.2
  59.5 0.9 %copy-done.2 = bf16[32,4096]{1,0:T(8,128)(2,1)S(1)} copy-done((bf16[32,4096]{1,0:T(8,128)(2,1)S(1)}, bf16[32,4096]{1,0:T(8,128)(2,1)}, u32[]{:S(2)}) %copy-start.2) | copy-done | bytes 262168
  60.5 1.5 %shard_map.138 = (bf16[32,4096]{1,0:T(8,128)(2,1)}, f32[64,2048]{1,0:T(8,128)}, f32[64,2048]{1,0:T(8,128)}, f32[64,1792]{1,0:T(8,128)}, f32[64,1792]{1,0:T(8,128)}) custom-call(bf16[32,4096]{1,0:T(8,128)(2,1)S(1)} %copy-done.2, bf16[2,4,64,512]{3,2,1,0:T(8,128)(2,1)S(1)} %copy-done.1, bf16[2,128,1792]{2,1,0:T(8,128)(2,1)S(1)} %copy-done), custom_call_target="tpu_custom_call" | custom-call | tf_op jit(solution)/shard_map/pallas_call | solution.py:557
Async XLA Ops:
  57.3 1.2 %copy-start = (bf16[2,128,1792]{2,1,0:T(8,128)(2,1)S(1)}, bf16[2,128,1792]{2,1,0:T(8,128)(2,1)}, u32[]{:S(2)}) copy-start(bf16[2,128,1792]{2,1,0:T(8,128)(2,1)} %get-tuple-element.15.b_all) | copy-start | bytes 2752516
  58.5 1.0 %copy-start.1 = (bf16[2,4,64,512]{3,2,1,0:T(8,128)(2,1)S(1)}, bf16[2,4,64,512]{3,2,1,0:T(8,128)(2,1)}, u32[]{:S(2)}) copy-start(bf16[2,4,64,512]{3,2,1,0:T(8,128)(2,1)} %get-tuple-element.14.a_all) | copy-start | bytes 1572868
  59.5 0.9 %copy-start.2 = (bf16[32,4096]{1,0:T(8,128)(2,1)S(1)}, bf16[32,4096]{1,0:T(8,128)(2,1)}, u32[]{:S(2)}) copy-start(bf16[32,4096]{1,0:T(8,128)(2,1)} %get-tuple-element.13.dx) | copy-start | bytes 786436
